TPU v7x, 256 devices: a whole 4x4x8 slice. The times are simulated.
256 devices in a mesh: branch: 2 (over core), seq: 16 (over x, z_lo), head: 8 (over y, z_hi).
Axes of the slice: x: 4, y: 4, z: 8 (z_hi: 2, z_lo: 4; z = z_hi * 4 + z_lo), core: 2. Of those that a mesh axis runs over, the one named last changes fastest.
Arguments:
- latent: float32 [8192, 3072], P(('seq', 'head')), may hold values from -8 to 8
- modulation: float32 [2, 3, 3072], P('branch'), may hold values from -1.2 to 1.2
- w_qkv: bfloat16 [3072, 24, 384], P(None, 'head'), may hold values from -5 to 5
- w_out: bfloat16 [24, 128, 3072], P('head'), may hold values from -0.5 to 0.5
- timestep: int32 [1], replicated, may hold values from 0 to 49
Outputs:
- stepped: float32 [8192, 3072], P(('seq', 'head'))
- denoised: float32 [8192, 3072], P(('seq', 'head'))
Inputs may be any that keep to these rules, and one draw needn't show every extreme that they name: `timestep`: one step index of the plan of 50 steps.
All inputs are finite; a program needn't handle non-finite values.
Results may differ from a plain program's by a relative error of at most 0.0055.
Values may be sent and summed in bfloat16 or wider, within the bound.
A program may use at most 128 MiB of HBM per device.

v0:
```python
import jax
import jax.numpy as jnp
from jax import lax
from jax.sharding import PartitionSpec as P

STEPS = 50


guidance_scale = 6.0
flow_shift = 7.0
epsilon = 1e-06


def sigma_at(step_value):
    fraction = 1.0 - step_value / STEPS
    return flow_shift * fraction / (1.0 + (flow_shift - 1.0) * fraction)


def modulate(latent, shift_vec, scale_vec):
    row_mean = jnp.mean(latent, axis=1, keepdims=True)
    centred = latent - row_mean
    row_var = jnp.mean(centred * centred, axis=1, keepdims=True)
    return (centred * lax.rsqrt(row_var + epsilon) * (1.0 + scale_vec) + shift_vec).astype(
        jnp.bfloat16
    )


def accumulate(carried, query_rows, key_block, value_block, score_scale):
    running_out, running_max, running_sum = carried
    scores = (
        jnp.einsum("hqd,khd->hqk", query_rows, key_block, preferred_element_type=jnp.float32)
        * score_scale
    )
    new_max = jnp.maximum(running_max, jnp.max(scores, axis=2))
    fade_factor = jnp.exp(running_max - new_max)
    expo = jnp.exp(scores - new_max[:, :, None])
    running_sum = running_sum * fade_factor + jnp.sum(expo, axis=2)
    running_out = running_out * fade_factor[:, :, None] + jnp.einsum(
        "hqk,khd->hqd", expo.astype(jnp.bfloat16), value_block, preferred_element_type=jnp.float32
    )
    return (running_out, new_max, running_sum)


def sweep(carried, query_rows, key_rows, value_rows, score_scale):
    key_count = key_rows.shape[0]
    block_len = 512

    def visit_block(step_index, inner):
        key_block = lax.dynamic_slice_in_dim(key_rows, step_index * block_len, block_len, 0)
        value_block = lax.dynamic_slice_in_dim(value_rows, step_index * block_len, block_len, 0)
        return accumulate(inner, query_rows, key_block, value_block, score_scale)

    return lax.fori_loop(0, key_count // block_len, visit_block, carried)


def shards(latent, modulation, w_qkv, w_out, timestep):
    tok_rows, model_width = latent.shape
    local_heads = w_qkv.shape[1]
    head_size = w_qkv.shape[2] // 3
    score_scale = head_size ** (-0.5)
    normed = modulate(latent, modulation[0, 0], modulation[0, 1])
    flat_in = w_qkv.reshape(model_width, local_heads * 3 * head_size)
    fetched = lax.all_gather(normed, "head", axis=0, tiled=True)
    projected = jnp.dot(fetched, flat_in, preferred_element_type=jnp.float32)
    qkv_all = projected.astype(jnp.bfloat16).reshape(fetched.shape[0], local_heads, 3 * head_size)
    block_rows = qkv_all.shape[0]
    query_rows = jnp.transpose(qkv_all[:, :, :head_size], (1, 0, 2))
    key_rows = qkv_all[:, :, head_size : 2 * head_size]
    value_rows = qkv_all[:, :, 2 * head_size :]
    start_state = (
        jnp.zeros((local_heads, block_rows, head_size), jnp.float32),
        jnp.full((local_heads, block_rows), -jnp.inf, jnp.float32),
        jnp.zeros((local_heads, block_rows), jnp.float32),
    )
    fetched = (
        lax.all_gather(key_rows, "seq", axis=0, tiled=True),
        lax.all_gather(value_rows, "seq", axis=0, tiled=True),
    )
    running_out, running_max, running_sum = sweep(
        start_state, query_rows, fetched[0], fetched[1], score_scale
    )
    attended = (running_out / running_sum[:, :, None]).astype(jnp.bfloat16)
    gate_vec = modulation[0, 2]
    branch_index = lax.axis_index("branch")
    branch_weight = jnp.where(branch_index == 0, guidance_scale, 1.0 - guidance_scale)
    moment = timestep[0].astype(jnp.float32)
    sigma_now = sigma_at(moment)
    step_size = sigma_at(moment + 1.0) - sigma_now
    head_total = lax.psum_scatter(
        jnp.einsum("hqd,hdc->qc", attended, w_out, preferred_element_type=jnp.float32),
        "head",
        scatter_dimension=0,
        tiled=True,
    )
    velocity = latent + lax.psum(branch_weight * gate_vec * head_total, "branch")
    return (latent + step_size * velocity, latent - sigma_now * velocity)


def solution(mesh):
    placed = (
        P(("seq", "head"), None),
        P("branch", None, None),
        P(None, "head", None),
        P("head", None, None),
        P(),
    )
    return jax.shard_map(
        shards,
        mesh=mesh,
        in_specs=placed,
        out_specs=(P(("seq", "head"), None), P(("seq", "head"), None)),
        check_vma=False,
    )
```

profile of v0, /device:TPU:7, one launch (start us, length us, event | category | flops | bytes accessed | tf_op | source)
XLA Modules:
  0.0 735.3 jit_solution(8475857700849991032)
XLA Ops:
  13.6 10.3 %copy.12 = bf16[3072,3,384]{0,2,1:T(8,128)(2,1)} copy(bf16[3072,3,384]{2,0,1:T(8,128)(2,1)} %param.9) | data formatting | bytes 14155776 | tf_op args[2]
  23.9 84.2 %all-gather.4.cloned.1.call-done = bf16[512,3072]{1,0:T(8,128)(2,1)} async-done(((bf16[64,3072]{1,0:T(8,128)(2,1)}), bf16[512,3072]{1,0:T(8,128)(2,1)}) %all-gather.4.cloned.1.call-update) | async-done | bytes 3145744 | tf_op jit(solution)/shard_map/all_gather | solution.py:63
  108.0 9.2 %convolution_convert_fusion = bf16[512,1152]{1,0:T(8,128)(2,1)} fusion(bf16[512,3072]{1,0:T(8,128)(2,1)} %all-gather.4.cloned.1.call-done, bf16[3072,1152]{0,1:T(8,128)(2,1)} %bitcast.35), kind=kOutput, calls=%fused_computation.21 | convolution fusion | flops 3624468480 | bytes 11403264 | tf_op jit(solution)/shard_map/dot_general | solution.py:64
  122.0 135.4 %all-gather.6.cloned.1.call-done = bf16[8192,3,128]{0,2,1:T(8,128)(2,1)} async-done(((bf16[512,3,128]{0,2,1:T(8,128)(2,1)}), bf16[8192,3,128]{0,2,1:T(8,128)(2,1)}) %all-gather.6.cloned.1.call-update) | async-done | bytes 6291472 | tf_op jit(solution)/shard_map/all_gather | solution.py:76
  257.4 143.7 %all-gather.8.cloned.1.call-done = bf16[8192,3,128]{0,2,1:T(8,128)(2,1)} async-done(((bf16[512,3,128]{0,2,1:T(8,128)(2,1)}), bf16[8192,3,128]{0,2,1:T(8,128)(2,1)}) %all-gather.8.cloned.1.call-update) | async-done | bytes 6291472 | tf_op jit(solution)/shard_map/all_gather | solution.py:77
  401.1 137.3 %while.18 = (s32[]{:T(128)}, f32[3,512,128]{2,1,0:T(8,128)S(1)}, f32[3,512]{1,0:T(4,128)S(1)}, f32[3,512]{1,0:T(4,128)}, bf16[8192,3,128]{0,2,1:T(8,128)(2,1)}, ...) while((s32[]{:T(128)}, f32[3,512,128]{2,1,0:T(8,128)S(1)}, ...), condition=%wide.region_5.0_spmd.clone, body=%wide.region_2.0_spmd.clone.sunk | while | flops 409542144 | bytes 24920320 | solution.py:53
  409.7 3.3 bitcast_reduce_fusion.2
  418.3 3.3 bitcast_reduce_fusion.2
  426.9 3.3 bitcast_reduce_fusion.2
  435.4 3.3 bitcast_reduce_fusion.2
  444.0 3.3 bitcast_reduce_fusion.2
  452.6 3.3 bitcast_reduce_fusion.2
  461.2 3.3 bitcast_reduce_fusion.2
  469.8 3.3 bitcast_reduce_fusion.2
  478.4 3.3 bitcast_reduce_fusion.2
  486.9 3.3 bitcast_reduce_fusion.2
  495.5 3.3 bitcast_reduce_fusion.2
  504.1 3.3 bitcast_reduce_fusion.2
  512.7 3.3 bitcast_reduce_fusion.2
  521.3 3.3 bitcast_reduce_fusion.2
  529.8 3.3 bitcast_reduce_fusion.2
  538.4 4.5 convolution_bitcast_fusion
  543.0 149.5 %reduce-scatter.2.cloned.1.call-done = f32[64,3072]{1,0:T(8,128)} async-done(((f32[512,3072]{1,0:T(8,128)}), f32[64,3072]{1,0:T(8,128)}) %reduce-scatter.2.cloned.1.call-update) | async-done | bytes 786448 | tf_op jit(solution)/shard_map/reduce_scatter | solution.py:89
  695.3 31.0 %all-reduce.2.cloned.1.call-done = f32[64,3072]{1,0:T(8,128)} async-done(((f32[64,3072]{1,0:T(8,128)}), f32[64,3072]{1,0:T(8,128)}) %all-reduce.2.cloned.1.call-update) | async-done | bytes 786448 | tf_op jit(solution)/shard_map/psum | solution.py:95
  (207 shorter events, 103.0 us)
Async XLA Ops:
  7.2 531.2 %copy-start = (bf16[3,128,3072]{2,1,0:T(8,128)(2,1)S(1)}, bf16[3,128,3072]{2,1,0:T(8,128)(2,1)}, u32[]{:S(2)}) copy-start(bf16[3,128,3072]{2,1,0:T(8,128)(2,1)} %param.10) | copy-start | bytes 7077892
  7.2 100.9 %all-gather.4.cloned.1.call-start = ((), (), s32[]{:S(2)}) async-start(), calls=%async_computation.1 | async-start | bytes 3538944 | tf_op jit(solution)/shard_map/all_gather | solution.py:63
  13.5 243.9 %all-gather.6.cloned.1.call-start = ((), (), s32[]{:S(2)}) async-start(), calls=%async_computation.2 | async-start | bytes 6684672 | tf_op jit(solution)/shard_map/all_gather | solution.py:76
  119.9 281.2 %all-gather.8.cloned.1.call-start = ((), (), s32[]{:S(2)}) async-start(), calls=%async_computation.3 | async-start | bytes 6684672 | tf_op jit(solution)/shard_map/all_gather | solution.py:77
  120.7 571.8 %reduce-scatter.2.cloned.1.call-start = ((), (), s32[]{:S(2)}) async-start(), calls=%async_computation.4 | async-start | bytes 7077888 | tf_op jit(solution)/shard_map/reduce_scatter | solution.py:89
  404.4 3.2 copy-start.1
  413.0 3.2 copy-start.1
  421.5 3.2 copy-start.1
  430.1 3.2 copy-start.1
  438.7 3.2 copy-start.1
  447.3 3.2 copy-start.1
  455.9 3.2 copy-start.1
  464.4 3.2 copy-start.1
  473.0 3.2 copy-start.1
  481.6 3.2 copy-start.1
  490.2 3.2 copy-start.1
  498.8 3.2 copy-start.1
  507.4 3.2 copy-start.1
  515.9 3.2 copy-start.1
  524.5 3.2 copy-start.1
  533.1 3.2 copy-start.1
  542.9 149.6 %copy-start.5 = (f32[1,1,3072]{2,0,1:T(1,128)S(1)}, f32[1,1,3072]{2,0,1:T(1,128)}, u32[]{:S(2)}) copy-start(f32[1,1,3072]{2,0,1:T(1,128)} %get-tuple-element.183) | copy-start | bytes 36868
  542.9 183.4 %copy-start.2 = (f32[64,3072]{1,0:T(8,128)S(1)}, f32[64,3072]{1,0:T(8,128)}, u32[]{:S(2)}) copy-start(f32[64,3072]{1,0:T(8,128)} %param.7) | copy-start | bytes 2359300
  542.9 183.4 %all-reduce.2.cloned.1.call-start = ((), (), s32[]{:S(2)}) async-start(), calls=%async_computation.5 | async-start | bytes 1572864 | tf_op jit(solution)/shard_map/psum | solution.py:95
  (32 other events, 51.1 us)
Sparse Core Ops, SparseCore 0:
  13.7 94.3 all-gather.3
  120.1 137.2 all-gather.5
  259.8 141.3 all-gather.7
  543.0 149.3 reduce-scatter.1
  695.7 30.6 all-reduce.1
where the time goes:
time: 738 us; the launch traced here: 735 us
  waiting for transfers between devices  545 us (74%)
  matrix products  98.8 us (13%)
  other arithmetic  52.4 us (7%)
  local copies, waits for them, and re-layouts  23.8 us (3%)
  between operations  14.6 us (2%)
    reduce_scatter x1, waiting for transfers between devices, shards(): lax.psum_scatter(jnp.einsum('hqd,hdc->qc', attended, w_out, preferred_ele...  150 us
    all_gather x1, waiting for transfers between devices, shards(): lax.all_gather(value_rows, 'seq', axis=0, tiled=True)  144 us
    all_gather x1, waiting for transfers between devices, shards(): lax.all_gather(key_rows, 'seq', axis=0, tiled=True)  135 us
    all_gather x1, waiting for transfers between devices, shards(): fetched = lax.all_gather(normed, 'head', axis=0, tiled=True)  84.2 us
    dot_general x16, matrix products, accumulate(): jnp.einsum('hqd,khd->hqk', query_rows, key_block, preferred_element_type=...  52.1 us
    reduce_sum x16, other arithmetic, accumulate(): running_sum = running_sum * fade_factor + jnp.sum(expo, axis=2)  41.2 us
    dot_general x16, matrix products, accumulate(): jnp.einsum('hqk,khd->hqd', expo.astype(jnp.bfloat16), value_block, prefer...  32.9 us
    psum x1, waiting for transfers between devices, shards(): lax.psum(branch_weight * gate_vec * head_total, 'branch')  31 us
  transfers between devices with their start and end apart: 5, of which 5 were waited for; matrix products, arithmetic and copies ran while one was open for 2% of the time, Pallas kernels for 0%

commit v1 on v0

v1 whole, which is shorter than its diff:
```python
import functools

import jax
import jax.numpy as jnp
from jax import lax
from jax.experimental import pallas as pl
from jax.experimental.pallas import tpu as pltpu
from jax.sharding import PartitionSpec as P

STEPS = 50
GUIDANCE = 6.0
SHIFT = 7.0
EPS = 1e-06
LOG2E = 1.4426950408889634
MESH = pl.DeviceIdType.MESH
F32, BF16 = jnp.float32, jnp.bfloat16

D = 3072
DH = 128
H = 3
NX, NY, NZ = 4, 4, 4
ROWS = 32
HALF = 2 * NY * ROWS
YD = (1, 3, 2)
XD = (1, 3, 2)
ZD = (2, 3, 1)


def sigma_at(step_value):
    fraction = 1.0 - step_value / STEPS
    return SHIFT * fraction / (1.0 + (SHIFT - 1.0) * fraction)


def toggled(z, k):
    if k == 1:
        return z + 1 - 2 * (z % 2)
    if k == 2:
        return z + 2 - 4 * (z // 2)
    return 3 - z


def kernel(
    lat_ref, mod_ref, wq_hbm, wo_hbm, out_ref,
    wq, wo, xh, nm, qb, kb, vb, osend, orecv, lsend, lrecv, att, attx, gate, gatex,
    psend, precv, zsend, zrecv, fin, finx,
    w_sem, xs_sem, xr_sem, g_sem, qs_sem, qr_sem, ks_sem, kr_sem, vs_sem, vr_sem,
    os_sem, or_sem, ls_sem, lr_sem, as_sem, ar_sem, ps_sem, pr_sem, e_sem,
):
    b, s, h = lax.axis_index("branch"), lax.axis_index("seq"), lax.axis_index("head")
    x, z, y, zh = s // NZ, s % NZ, h // 2, h % 2

    def to_y(d):
        return (b, s, ((y + d) % NY) * 2 + zh)

    def to_x(d):
        return (b, ((x + d) % NX) * NZ + z, h)

    def to_z(k):
        return (b, x * NZ + toggled(z, k), h)

    far = (b, s, h + 1 - 2 * zh)
    twin = (1 - b, s, h)

    def remote(src, dst, ssem, rsem, dev):
        return pltpu.make_async_remote_copy(
            src_ref=src, dst_ref=dst, send_sem=ssem, recv_sem=rsem,
            device_id=dev, device_id_type=MESH,
        )

    load_q = pltpu.make_async_copy(wq_hbm, wq, w_sem.at[0])
    load_o = pltpu.make_async_copy(wo_hbm, wo, w_sem.at[1])
    load_q.start()
    load_o.start()

    barrier = pltpu.get_barrier_semaphore()
    peers = [to_y(d) for d in YD] + [to_x(d) for d in XD] + [to_z(k) for k in ZD] + [far, twin]
    for dev in peers:
        pl.semaphore_signal(barrier, inc=1, device_id=dev, device_id_type=MESH)

    def normalise(at):
        rows = lat_ref[pl.ds(pl.multiple_of(at * ROWS, ROWS), ROWS), :]
        centred = rows - jnp.mean(rows, axis=1, keepdims=True)
        var = jnp.mean(centred * centred, axis=1, keepdims=True)
        return (centred * lax.rsqrt(var + EPS)).astype(BF16)

    xh[0, 0, 0] = normalise(b)
    weight = jnp.where(b == 0, GUIDANCE, 1.0 - GUIDANCE).astype(F32)
    gate[...] = jnp.broadcast_to(weight * mod_ref[2:3, :], gate.shape)
    pl.semaphore_wait(barrier, len(peers))

    sends = []

    def go(copy):
        copy.start()
        sends.append(copy)
        return copy

    def x_copy(src, dst, dev):
        return remote(xh.at[src], xh.at[dst], xs_sem.at[dst], xr_sem.at[dst], dev)

    own = (0, 0, 0)
    from_far = go(x_copy(own, (1, 0, 0), far))
    from_y = [go(x_copy(own, (0, 0, d), to_y(d))) for d in YD]
    from_twin0, from_twin1 = [], []
    gate_copy = go(remote(gate, gatex, g_sem.at[0], g_sem.at[1], twin))
    xh[0, 1, 0] = normalise(1 - b)
    for d, copy in zip(YD, from_y):
        copy.wait_recv()
        from_twin0.append(go(x_copy((0, 0, d), (0, 1, d), twin)))
    from_far.wait_recv()
    from_y = [go(x_copy((1, 0, 0), (1, 0, d), to_y(d))) for d in YD]
    from_twin1.append(go(x_copy((1, 0, 0), (1, 1, 0), twin)))

    shift, scale = mod_ref[0:1, :], 1.0 + mod_ref[1:2, :]
    q_scale = DH**-0.5 * LOG2E
    q_in, kv_in = {}, {}

    def project(dz):
        for half in range(2):
            for dy in range(NY):
                nm[pl.ds((half * NY + dy) * ROWS, ROWS), :] = (
                    xh[dz, half, dy].astype(F32) * scale + shift
                ).astype(BF16)

        def per_head(i, carry):
            got = jnp.dot(nm[...], wq[i], preferred_element_type=F32)
            qb[0, dz, i] = (got[:, :DH] * q_scale).astype(BF16)
            kb[0, dz, i] = got[:, DH : 2 * DH].T.astype(BF16)
            vb[0, dz, i] = got[:, 2 * DH :].astype(BF16)
            return carry

        lax.fori_loop(0, H, per_head, 0)
        for d in XD:
            kv_in[d, dz, 0] = go(remote(kb.at[0, dz], kb.at[d, dz], ks_sem.at[d, dz], kr_sem.at[d, dz], to_x(d)))
            kv_in[d, dz, 1] = go(remote(vb.at[0, dz], vb.at[d, dz], vs_sem.at[d, dz], vr_sem.at[d, dz], to_x(d)))
        for k in ZD:
            q_in[k, dz] = go(remote(qb.at[0, dz], qb.at[k, dz], qs_sem.at[k, dz], qr_sem.at[k, dz], to_z(k)))

    for copy in from_twin0:
        copy.wait_recv()
    load_q.wait()
    project(0)
    for d, copy in zip(YD, from_y):
        copy.wait_recv()
        from_twin1.append(go(x_copy((1, 0, d), (1, 1, d), twin)))
    for copy in from_twin1:
        copy.wait_recv()
    project(1)

    for copy in kv_in.values():
        copy.wait_recv()

    lane = lax.broadcasted_iota(jnp.int32, (HALF, DH), 1)

    def attend(k, dz):
        packed = jnp.zeros((HALF, DH), F32)
        for i in range(H):
            query = qb[k, dz, i]
            scores = jnp.concatenate(
                [
                    jnp.dot(query, kb[d, e, i], preferred_element_type=F32)
                    for d in range(NX)
                    for e in range(2)
                ],
                axis=1,
            )
            peak = jnp.max(scores, axis=1, keepdims=True)
            expo = jnp.exp2(scores - peak)
            total = jnp.sum(expo, axis=1, keepdims=True)
            probs = expo.astype(BF16)
            mixed = jnp.zeros((HALF, DH), F32)
            for d in range(NX):
                for e in range(2):
                    at = (d * 2 + e) * HALF
                    mixed += jnp.dot(probs[:, at : at + HALF], vb[d, e, i], preferred_element_type=F32)
            osend[k, dz, i] = (mixed / total).astype(BF16)
            packed = jnp.where(lane == i, peak + jnp.log2(total), packed)
        lsend[k, dz] = packed.T[:8, :]

    o_in, l_in = {}, {}
    for k in ZD + (0,):
        if k:
            for dz in range(2):
                q_in[k, dz].wait_recv()

        def per_dz(i, carry, k=k):
            attend(k, 1 - i)
            return carry

        lax.fori_loop(0, 2, per_dz, 0)
        if k:
            for dz in (1, 0):
                o_in[k, dz] = go(remote(osend.at[k, dz], orecv.at[k, dz], os_sem.at[k, dz], or_sem.at[k, dz], to_z(k)))
                l_in[k, dz] = go(remote(lsend.at[k, dz], lrecv.at[k, dz], ls_sem.at[k, dz], lr_sem.at[k, dz], to_z(k)))

    load_o.wait()
    gate_copy.wait_recv()

    def merge(dz):
        logs = [
            jnp.concatenate([ref, jnp.zeros((DH - 8, HALF), F32)], axis=0).T
            for ref in [lsend[0, dz]] + [lrecv[k, dz] for k in ZD]
        ]
        peak = functools.reduce(jnp.maximum, logs)
        parts = [jnp.exp2(log - peak) for log in logs]
        total = functools.reduce(jnp.add, parts)
        for i in range(H):
            mixed = jnp.zeros((HALF, DH), F32)
            for part, ref in zip(parts, [osend.at[0]] + [orecv.at[k] for k in ZD]):
                mixed += (part / total)[:, i : i + 1] * ref[dz, i].astype(F32)
            mixed = mixed.astype(BF16)
            att[dz, 0, :, i * DH : (i + 1) * DH] = mixed[: HALF // 2]
            att[dz, 1, :, i * DH : (i + 1) * DH] = mixed[HALF // 2 :]
        return go(remote(att.at[dz, 1], attx.at[dz], as_sem.at[dz], ar_sem.at[dz], twin))

    a_in = {}
    for dz in (1, 0):
        for k in ZD:
            o_in[k, dz].wait_recv()
            l_in[k, dz].wait_recv()
        a_in[dz] = merge(dz)

    p_in = {}
    wide = 512
    for dz in (1, 0):
        a_in[dz].wait_recv()

        def per_tile(t, carry, dz=dz):
            cols = pl.ds(pl.multiple_of(t * wide, wide), wide)
            tile = gate[0:1, cols] * jnp.dot(att[dz, 0], wo[:, cols], preferred_element_type=F32)
            tile += gatex[0:1, cols] * jnp.dot(attx[dz], wo[:, cols], preferred_element_type=F32)
            psend[dz, :, :, cols] = tile.astype(BF16).reshape(NY, ROWS, wide)
            return carry

        lax.fori_loop(0, D // wide, per_tile, 0)
        for d in YD:
            p_in[dz, d] = go(remote(psend.at[dz, d], precv.at[dz, d], ps_sem.at[dz, d], pr_sem.at[dz, d], to_y(NY - d)))

    def summed(dz):
        total = psend[dz, 0].astype(F32)
        for d in YD:
            p_in[dz, d].wait_recv()
            total += precv[dz, d].astype(F32)
        return total

    zsend[...] = summed(1).astype(BF16)
    z_copy = go(remote(zsend, zrecv, e_sem.at[0], e_sem.at[1], far))
    fin[...] = summed(0)
    z_copy.wait_recv()
    fin[...] += zrecv[...].astype(F32)
    f_copy = go(remote(fin, finx, e_sem.at[2], e_sem.at[3], twin))
    out_ref[pl.ds(pl.multiple_of(b * ROWS, ROWS), ROWS), :] = fin[...]
    f_copy.wait_recv()
    out_ref[pl.ds(pl.multiple_of((1 - b) * ROWS, ROWS), ROWS), :] = finx[...]

    for copy in sends:
        copy.wait_send()


def guided(latent, modulation, wq, wo):
    dma = pltpu.SemaphoreType.DMA
    vmem = pltpu.VMEM
    scratch = [
        vmem((H, D, 3 * DH), BF16),
        vmem((H * DH, D), BF16),
        vmem((2, 2, NY, ROWS, D), BF16),
        vmem((HALF, D), BF16),
        vmem((NZ, 2, H, HALF, DH), BF16),
        vmem((NX, 2, H, DH, HALF), BF16),
        vmem((NX, 2, H, HALF, DH), BF16),
        vmem((NZ, 2, H, HALF, DH), BF16),
        vmem((NZ, 2, H, HALF, DH), BF16),
        vmem((NZ, 2, 8, HALF), F32),
        vmem((NZ, 2, 8, HALF), F32),
        vmem((2, 2, HALF // 2, H * DH), BF16),
        vmem((2, HALF // 2, H * DH), BF16),
        vmem((8, D), F32),
        vmem((8, D), F32),
        vmem((2, NY, ROWS, D), BF16),
        vmem((2, NY, ROWS, D), BF16),
        vmem((ROWS, D), BF16),
        vmem((ROWS, D), BF16),
        vmem((ROWS, D), F32),
        vmem((ROWS, D), F32),
        dma((2,)),
        dma((2, 2, NY)), dma((2, 2, NY)),
        dma((2,)),
        dma((NZ, 2)), dma((NZ, 2)),
        dma((NX, 2)), dma((NX, 2)),
        dma((NX, 2)), dma((NX, 2)),
        dma((NZ, 2)), dma((NZ, 2)),
        dma((NZ, 2)), dma((NZ, 2)),
        dma((2,)), dma((2,)),
        dma((2, NY)), dma((2, NY)),
        dma((4,)),
    ]
    held = pl.BlockSpec(memory_space=pltpu.VMEM)
    left = pl.BlockSpec(memory_space=pl.ANY)
    return pl.pallas_call(
        kernel,
        out_shape=jax.ShapeDtypeStruct(latent.shape, F32),
        in_specs=[held, held, left, left],
        out_specs=held,
        scratch_shapes=scratch,
        compiler_params=pltpu.CompilerParams(
            collective_id=0, has_side_effects=True, vmem_limit_bytes=60 * 1024 * 1024
        ),
    )(latent, modulation, wq, wo)


def shards(latent, modulation, w_qkv, w_out, timestep):
    wq = jnp.transpose(w_qkv, (1, 0, 2))
    wo = w_out.reshape(H * DH, D)
    change = guided(latent, modulation.reshape(3, D), wq, wo)
    moment = timestep[0].astype(F32)
    sigma_now = sigma_at(moment)
    step_size = sigma_at(moment + 1.0) - sigma_now
    velocity = latent + change
    return (latent + step_size * velocity, latent - sigma_now * velocity)


def solution(mesh):
    placed = (
        P(("seq", "head"), None),
        P("branch", None, None),
        P(None, "head", None),
        P("head", None, None),
        P(),
    )
    return jax.shard_map(
        shards,
        mesh=mesh,
        in_specs=placed,
        out_specs=(P(("seq", "head"), None), P(("seq", "head"), None)),
        check_vma=False,
    )
```

time: 738 us -> 139 us (0.19)
  the two profiles are of different devices: /device:TPU:7 before, /device:TPU:1 now
where the time goes in v1:
time: 139 us
  Pallas kernels  134 us (96%)
  other arithmetic  2.47 us (2%)
  between operations  1.47 us (1%)
  local copies, waits for them, and re-layouts  1.41 us (1%)
    pallas_call x1, Pallas kernels, guided(): pl.pallas_call(kernel, out_shape=jax.ShapeDtypeStruct(latent.shape, F32),...  134 us

profile of v1, /device:TPU:1, one launch (start us, length us, event | category | flops | bytes accessed | tf_op | source)
XLA Modules:
  0.0 139.2 jit_solution(12933410330309706217)
XLA Ops:
  0.6 0.0 copy-start
  1.5 1.4 %copy.9 = f32[1,3,3072]{2,1,0:T(4,128)} copy(f32[1,3,3072]{2,0,1:T(1,128)} %param.6) | data formatting | bytes 73728
  2.9 133.9 %shard_map.68 = f32[64,3072]{1,0:T(8,128)} custom-call(f32[64,3072]{1,0:T(8,128)} %lat_ref.1, f32[3,3072]{1,0:T(4,128)} %bitcast.9, bf16[3,3072,384]{2,1,0:T(8,128)(2,1)} %bitcast.7, bf16[384,3072]{1,0:T(8,128)(2,1)} %bitcast.8), custom_call_target="tpu_custom_call" | custom-call | tf_op jit(solution)/shard_map/pallas_call | solution.py:299
  136.7 0.0 copy-done
  136.7 2.5 %multiply_subtract_fusion = (f32[64,3072]{1,0:T(8,128)}, f32[64,3072]{1,0:T(8,128)}) fusion(f32[64,3072]{1,0:T(8,128)S(1)} %copy-done, f32[]{:T(128)} %bitcast.1, f32[64,3072]{1,0:T(8,128)} %shard_map.68, f32[]{:T(128)S(6)} %sub.19), kind=kLoop, calls=%fused_computation | loop fusion | flops 983040 | bytes 3145736 | tf_op jit(solution)/shard_map/sub | solution.py:319
Async XLA Ops:
  0.6 136.1 %copy-start = (f32[64,3072]{1,0:T(8,128)S(1)}, f32[64,3072]{1,0:T(8,128)}, u32[]{:S(2)}) copy-start(f32[64,3072]{1,0:T(8,128)} %lat_ref.1) | copy-start | bytes 2359300

commit v2 on v1

v2 whole, which is shorter than its diff:
```python
import functools

import jax
import jax.numpy as jnp
from jax import lax
from jax.experimental import pallas as pl
from jax.experimental.pallas import tpu as pltpu
from jax.sharding import PartitionSpec as P

STEPS = 50
GUIDANCE = 6.0
SHIFT = 7.0
EPS = 1e-06
LOG2E = 1.4426950408889634
MESH = pl.DeviceIdType.MESH
F32, BF16 = jnp.float32, jnp.bfloat16

D = 3072
DH = 128
H = 3
NX, NY, NZ = 4, 4, 4
ROWS = 32
HALF = 2 * NY * ROWS
YD = (1, 3, 2)
XD = (1, 3, 2)
ZD = (2, 3, 1)


def sigma_at(step_value):
    fraction = 1.0 - step_value / STEPS
    return SHIFT * fraction / (1.0 + (SHIFT - 1.0) * fraction)


def toggled(z, k):
    if k == 1:
        return z + 1 - 2 * (z % 2)
    if k == 2:
        return z + 2 - 4 * (z // 2)
    return 3 - z


def kernel(
    lat_ref, mod_ref, wq_hbm, wo_hbm, out_ref,
    wq, wo, xh, nm, qb, kv, osend, orecv, lsend, lrecv, att, attx, gate, gatex,
    psend, precv, zsend, zrecv, fin, finx,
    w_sem, xs_sem, xr_sem, g_sem, qs_sem, qr_sem, q3_sem, ks_sem, kr_sem, k2_sem,
    os_sem, or_sem, ls_sem, lr_sem, as_sem, ar_sem, ps_sem, pr_sem, zs_sem, zr_sem, fs_sem, fr_sem,
):
    b, s, h = lax.axis_index("branch"), lax.axis_index("seq"), lax.axis_index("head")
    x, z, y, zh = s // NZ, s % NZ, h // 2, h % 2

    def to_y(d):
        return (b, s, ((y + d) % NY) * 2 + zh)

    def to_x(d):
        return (b, ((x + d) % NX) * NZ + z, h)

    def to_z(k):
        return (b, x * NZ + toggled(z, k), h)

    far = (b, s, h + 1 - 2 * zh)
    twin = (1 - b, s, h)
    inner = (z == 1) | (z == 2)

    def remote(src, dst, ssem, rsem, dev):
        return pltpu.make_async_remote_copy(
            src_ref=src, dst_ref=dst, send_sem=ssem, recv_sem=rsem,
            device_id=dev, device_id_type=MESH,
        )

    load_q = pltpu.make_async_copy(wq_hbm, wq, w_sem.at[0])
    load_o = pltpu.make_async_copy(wo_hbm, wo, w_sem.at[1])
    load_q.start()
    load_o.start()

    barrier = pltpu.get_barrier_semaphore()
    peers = [to_y(d) for d in YD] + [to_x(d) for d in XD] + [to_z(k) for k in ZD] + [far, twin]
    for dev in peers:
        pl.semaphore_signal(barrier, inc=1, device_id=dev, device_id_type=MESH)

    def normalise(at):
        rows = lat_ref[pl.ds(pl.multiple_of(at * ROWS, ROWS), ROWS), :]
        centred = rows - jnp.mean(rows, axis=1, keepdims=True)
        var = jnp.mean(centred * centred, axis=1, keepdims=True)
        return (centred * lax.rsqrt(var + EPS)).astype(BF16).reshape(2, ROWS // 2, D)

    xh[0, 0, 0] = normalise(b)
    weight = jnp.where(b == 0, GUIDANCE, 1.0 - GUIDANCE).astype(F32)
    gate[...] = jnp.broadcast_to(weight * mod_ref[2], gate.shape)
    pl.semaphore_wait(barrier, len(peers))

    sends = []

    def go(copy):
        copy.start()
        sends.append(copy)
        return copy

    def x_copy(src, dst, dev):
        return go(remote(xh.at[src], xh.at[dst], xs_sem.at[dst], xr_sem.at[dst], dev))

    x_in = {}

    def spread(dz, c):
        for d in (1, 3):
            x_in[dz, 0, d, c] = x_copy((dz, 0, 0, c), (dz, 0, d, c), to_y(d))

    def pass_on(dz, d, c):
        x_in[dz, 0, d, c].wait_recv()
        if (d, c) in ((1, 0), (3, 1)):
            x_in[dz, 0, 2, c] = x_copy((dz, 0, d, c), (dz, 0, 2, c), to_y(d))
        x_in[dz, 1, d, c] = x_copy((dz, 0, d, c), (dz, 1, d, c), twin)

    for c in range(2):
        x_in[1, 0, 0, c] = x_copy((0, 0, 0, c), (1, 0, 0, c), far)
        spread(0, c)
    gate_copy = go(remote(gate, gatex, g_sem.at[0], g_sem.at[1], twin))
    xh[0, 1, 0] = normalise(1 - b)

    pass_on(0, 1, 0)
    pass_on(0, 3, 0)
    x_in[1, 0, 0, 0].wait_recv()
    spread(1, 0)
    x_in[1, 1, 0, 0] = x_copy((1, 0, 0, 0), (1, 1, 0, 0), twin)
    pass_on(0, 3, 1)
    pass_on(0, 1, 1)
    x_in[1, 0, 0, 1].wait_recv()
    spread(1, 1)
    x_in[1, 1, 0, 1] = x_copy((1, 0, 0, 1), (1, 1, 0, 1), twin)
    pass_on(0, 2, 0)
    pass_on(0, 2, 1)

    q_scale = DH**-0.5 * LOG2E
    q_in, kv_in = {}, {}

    def project(dz):
        for half in range(2):
            for dy in range(NY):
                if (half, dy) == (1, 0) and dz == 0:
                    continue
                if half == 1:
                    for c in range(2):
                        x_in[dz, 1, dy, c].wait_recv()
        for half in range(2):
            for dy in range(NY):
                nm[pl.ds((half * NY + dy) * ROWS, ROWS), :] = (
                    xh[dz, half, dy].reshape(ROWS, D).astype(F32) * (1.0 + mod_ref[1]) + mod_ref[0]
                ).astype(BF16)
        for i in range(H):
            got = jnp.dot(nm[...], wq[i], preferred_element_type=F32)
            qb[0, i, dz] = (got[:, :DH] * q_scale).astype(BF16)
            for j in range(2):
                rows = slice(j * DH, (j + 1) * DH)
                kv[0, i, dz, j] = got[rows, DH : 2 * DH].T.astype(BF16)
                kv[0, i, dz, 2 + j] = got[rows, 2 * DH :].astype(BF16)
            for d in (1, 3):
                at = (d, i, dz)
                kv_in[at] = go(remote(kv.at[0, i, dz], kv.at[at], ks_sem.at[at], kr_sem.at[at], to_x(d)))
            for k in (2, 1):
                q_in[k, i, dz] = go(
                    remote(qb.at[0, i, dz], qb.at[k, i, dz], qs_sem.at[k, i, dz], qr_sem.at[k, i, dz], to_z(k))
                )
            near = remote(qb.at[0, i, dz], qb.at[3, i, dz], qs_sem.at[3, i, dz], qr_sem.at[3, i, dz], to_z(3))
            q_in[3, i, dz] = near
            pl.when(inner)(near.start)

    def relay_x(dz, i):
        for d, first in ((1, 0), (3, 2)):
            kv_in[d, i, dz].wait_recv()
            half = pl.ds(first, 2)
            kv_in[2, i, dz, first] = go(
                remote(
                    kv.at[d, i, dz, half],
                    kv.at[2, i, dz, half],
                    k2_sem.at[0, i, dz, first // 2],
                    k2_sem.at[1, i, dz, first // 2],
                    to_x(d),
                )
            )

    relays = []

    def relay_z(dz, i):
        q_in[2, i, dz].wait_recv()
        relay = remote(qb.at[2, i, dz], qb.at[3, i, dz], q3_sem.at[i, dz], qr_sem.at[3, i, dz], to_z(1))
        pl.when(inner)(relay.start)
        relays.append(relay)

    load_q.wait()
    project(0)
    pass_on(1, 1, 0)
    pass_on(1, 3, 0)
    relay_x(0, 0)
    pass_on(1, 3, 1)
    pass_on(1, 1, 1)
    relay_x(0, 1)
    relay_z(0, 0)
    pass_on(1, 2, 0)
    pass_on(1, 2, 1)
    relay_x(0, 2)
    relay_z(0, 1)
    project(1)
    relay_z(0, 2)
    for i in range(H):
        relay_x(1, i)
        relay_z(1, i)

    def attend(k, i, e):
        query = qb[k, i, e]
        scores = jnp.concatenate(
            [
                jnp.dot(
                    query,
                    jnp.concatenate([kv[d, i, f, 0], kv[d, i, f, 1]], axis=1),
                    preferred_element_type=F32,
                )
                for d in range(NX)
                for f in range(2)
            ],
            axis=1,
        )
        peak = jnp.max(scores, axis=1, keepdims=True)
        expo = jnp.exp2(scores - peak)
        total = jnp.sum(expo, axis=1, keepdims=True)
        probs = expo.astype(BF16)
        mixed = jnp.zeros((HALF, DH), F32)
        for d in range(NX):
            for f in range(2):
                at = (d * 2 + f) * HALF
                mixed += jnp.dot(
                    probs[:, at : at + HALF], kv[d, i, f, 2:4].reshape(HALF, DH), preferred_element_type=F32
                )
        osend[k, i, e] = (mixed / total).astype(BF16)
        lsend[k, i, e] = jnp.broadcast_to(peak + jnp.log2(total), (HALF, DH)).T[:8, :]

    o_in = {}

    def send_back(k, i, e, slot, dev):
        at = (slot, i, e)
        o_in[at] = [
            go(remote(osend.at[k, i, e], orecv.at[at], os_sem.at[at], or_sem.at[at], dev)),
            go(remote(lsend.at[k, i, e], lrecv.at[at], ls_sem.at[at], lr_sem.at[at], dev)),
        ]

    def merged(parts):
        logs = [log[...] for _, log in parts]
        peak = functools.reduce(jnp.maximum, logs)
        shares = [jnp.exp2(log - peak) for log in logs]
        total = functools.reduce(jnp.add, shares)
        mixed = jnp.zeros((HALF, DH), F32)
        for share, (out, _) in zip(shares, parts):
            spread_out = jnp.concatenate([share / total] * (DH // 8), axis=0).T
            mixed += spread_out * out[...].astype(F32)
        return mixed.astype(BF16), peak + jnp.log2(total)

    def cross(i, e):
        for copy in o_in[3, i, e]:
            copy.wait_recv()
        out, log = merged(
            [(osend.at[2, i, e], lsend.at[2, i, e]), (orecv.at[3, i, e], lrecv.at[3, i, e])]
        )
        osend[4, i, e] = out
        lsend[4, i, e] = log
        send_back(4, i, e, 2, to_z(2))

    def merge(i, e):
        for k in (1, 2):
            for copy in o_in[k, i, e]:
                copy.wait_recv()
        out, _ = merged(
            [(osend.at[0, i, e], lsend.at[0, i, e])]
            + [(orecv.at[k, i, e], lrecv.at[k, i, e]) for k in (1, 2)]
        )
        att[e, 0, :, i * DH : (i + 1) * DH] = out[: HALF // 2]
        att[e, 1, :, i * DH : (i + 1) * DH] = out[HALF // 2 :]

    def outgoing(i, e):
        for k in (3, 1):
            q_in[k, i, e].wait_recv()
            attend(k, i, e)
            send_back(k, i, e, k, to_z(1))

    def staying(i, e):
        attend(2, i, e)
        attend(0, i, e)

    a_in, p_in = {}, {}
    wide = D // 2
    tile = 512

    def exchange(dz):
        for i in range(H):
            merge(i, dz)
        a_in[dz] = go(remote(att.at[dz, 1], attx.at[dz], as_sem.at[dz], ar_sem.at[dz], twin))

    def project_out(dz):
        a_in[dz].wait_recv()
        for c in range(2):
            for t in range(wide // tile):
                cols = slice(c * wide + t * tile, c * wide + (t + 1) * tile)
                part = gate[0:1, cols] * jnp.dot(att[dz, 0], wo[:, cols], preferred_element_type=F32)
                part += gatex[0:1, cols] * jnp.dot(attx[dz], wo[:, cols], preferred_element_type=F32)
                psend[dz, c, :, :, t * tile : (t + 1) * tile] = part.astype(BF16).reshape(NY, ROWS, tile)
            for d in (2, 1, 3):
                at = (dz, c, d)
                p_in[at] = go(remote(psend.at[at], precv.at[at], ps_sem.at[at], pr_sem.at[at], to_y(NY - d)))

    before = None
    for e in (1, 0):
        for i in range(H):
            if e == 1:
                for dz in range(2):
                    for first in (0, 2):
                        kv_in[2, i, dz, first].wait_recv()
            outgoing(i, e)
            if before:
                cross(*before)
            before = (i, e)
            if (i, e) == (2, 0):
                project_out(1)
            staying(i, e)
            if (i, e) == (1, 0):
                load_o.wait()
                gate_copy.wait_recv()
                exchange(1)
    cross(*before)

    def summed(dz, c):
        total = psend[dz, c, 0].astype(F32)
        for d in YD:
            p_in[dz, c, d].wait_recv()
            total += precv[dz, c, d].astype(F32)
        return total

    z_in, f_in = [], []
    for c in range(2):
        zsend[c] = summed(1, c).astype(BF16)
        z_in.append(go(remote(zsend.at[c], zrecv.at[c], zs_sem.at[c], zr_sem.at[c], far)))
    exchange(0)
    project_out(0)
    for c in range(2):
        whole = summed(0, c)
        z_in[c].wait_recv()
        whole += zrecv[c].astype(F32)
        fin[c] = whole
        f_in.append(go(remote(fin.at[c], finx.at[c], fs_sem.at[c], fr_sem.at[c], twin)))
        out_ref[pl.ds(pl.multiple_of(b * ROWS, ROWS), ROWS), c * wide : (c + 1) * wide] = whole
    for c in range(2):
        f_in[c].wait_recv()
        out_ref[pl.ds(pl.multiple_of((1 - b) * ROWS, ROWS), ROWS), c * wide : (c + 1) * wide] = finx[c]

    for copy in sends:
        copy.wait_send()

    @pl.when(inner)
    def _():
        for copy in relays:
            copy.wait_send()
        for i in range(H):
            for dz in range(2):
                q_in[3, i, dz].wait_send()


def guided(latent, modulation, wq, wo):
    dma = pltpu.SemaphoreType.DMA
    vmem = pltpu.VMEM
    scratch = [
        vmem((H, D, 3 * DH), BF16),
        vmem((H * DH, D), BF16),
        vmem((2, 2, NY, 2, ROWS // 2, D), BF16),
        vmem((HALF, D), BF16),
        vmem((NZ, H, 2, HALF, DH), BF16),
        vmem((NX, H, 2, 4, DH, DH), BF16),
        vmem((NZ + 1, H, 2, HALF, DH), BF16),
        vmem((NZ, H, 2, HALF, DH), BF16),
        vmem((NZ + 1, H, 2, 8, HALF), F32),
        vmem((NZ, H, 2, 8, HALF), F32),
        vmem((2, 2, HALF // 2, H * DH), BF16),
        vmem((2, HALF // 2, H * DH), BF16),
        vmem((8, D), F32),
        vmem((8, D), F32),
        vmem((2, 2, NY, ROWS, D // 2), BF16),
        vmem((2, 2, NY, ROWS, D // 2), BF16),
        vmem((2, ROWS, D // 2), BF16),
        vmem((2, ROWS, D // 2), BF16),
        vmem((2, ROWS, D // 2), F32),
        vmem((2, ROWS, D // 2), F32),
        dma((2,)),
        dma((2, 2, NY, 2)), dma((2, 2, NY, 2)),
        dma((2,)),
        dma((NZ, H, 2)), dma((NZ, H, 2)), dma((H, 2)),
        dma((NX, H, 2)), dma((NX, H, 2)), dma((2, H, 2, 2)),
        dma((NZ, H, 2)), dma((NZ, H, 2)),
        dma((NZ, H, 2)), dma((NZ, H, 2)),
        dma((2,)), dma((2,)),
        dma((2, 2, NY)), dma((2, 2, NY)),
        dma((2,)), dma((2,)),
        dma((2,)), dma((2,)),
    ]
    held = pl.BlockSpec(memory_space=pltpu.VMEM)
    left = pl.BlockSpec(memory_space=pl.ANY)
    return pl.pallas_call(
        kernel,
        out_shape=jax.ShapeDtypeStruct(latent.shape, F32),
        in_specs=[held, held, left, left],
        out_specs=held,
        scratch_shapes=scratch,
        compiler_params=pltpu.CompilerParams(
            collective_id=0, has_side_effects=True, vmem_limit_bytes=60 * 1024 * 1024
        ),
    )(latent, modulation, wq, wo)


def shards(latent, modulation, w_qkv, w_out, timestep):
    wq = jnp.transpose(w_qkv, (1, 0, 2))
    wo = w_out.reshape(H * DH, D)
    change = guided(latent, jnp.transpose(modulation, (1, 0, 2)), wq, wo)
    moment = timestep[0].astype(F32)
    sigma_now = sigma_at(moment)
    step_size = sigma_at(moment + 1.0) - sigma_now
    velocity = latent + change
    return (latent + step_size * velocity, latent - sigma_now * velocity)


def solution(mesh):
    placed = (
        P(("seq", "head"), None),
        P("branch", None, None),
        P(None, "head", None),
        P("head", None, None),
        P(),
    )
    return jax.shard_map(
        shards,
        mesh=mesh,
        in_specs=placed,
        out_specs=(P(("seq", "head"), None), P(("seq", "head"), None)),
        check_vma=False,
    )
```

time: 139 us -> 116 us (0.83)
  the two profiles are of different devices: /device:TPU:1 before, /device:TPU:7 now
where the time goes in v2:
time: 116 us
  Pallas kernels  112 us (97%)
  other arithmetic  2.47 us (2%)
  between operations  1.47 us (1%)
    pallas_call x1, Pallas kernels, guided(): pl.pallas_call(kernel, out_shape=jax.ShapeDtypeStruct(latent.shape, F32),...  112 us
    sub x1, other arithmetic, shards(): return (latent + step_size * velocity, latent - sigma_now * velocity)  2.47 us

profile of v2, /device:TPU:7, one launch (start us, length us, event | category | flops | bytes accessed | tf_op | source)
XLA Modules:
  0.0 116.3 jit_solution(16502746065923464651)
XLA Ops:
  0.6 0.0 copy-start
  1.5 112.4 %shard_map.68 = f32[64,3072]{1,0:T(8,128)} custom-call(f32[64,3072]{1,0:T(8,128)} %lat_ref.1, f32[3,1,3072]{2,1,0:T(1,128)} %bitcast.7, bf16[3,3072,384]{2,1,0:T(8,128)(2,1)} %bitcast.5, bf16[384,3072]{1,0:T(8,128)(2,1)} %bitcast.6), custom_call_target="tpu_custom_call" | custom-call | tf_op jit(solution)/shard_map/pallas_call | solution.py:402
  113.8 0.0 copy-done
  113.8 2.5 %multiply_subtract_fusion = (f32[64,3072]{1,0:T(8,128)}, f32[64,3072]{1,0:T(8,128)}) fusion(f32[64,3072]{1,0:T(8,128)S(1)} %copy-done, f32[]{:T(128)} %bitcast.1, f32[64,3072]{1,0:T(8,128)} %shard_map.68, f32[]{:T(128)S(6)} %sub.19), kind=kLoop, calls=%fused_computation | loop fusion | flops 983040 | bytes 3145736 | tf_op jit(solution)/shard_map/sub | solution.py:422
Async XLA Ops:
  0.6 113.2 %copy-start = (f32[64,3072]{1,0:T(8,128)S(1)}, f32[64,3072]{1,0:T(8,128)}, u32[]{:S(2)}) copy-start(f32[64,3072]{1,0:T(8,128)} %lat_ref.1) | copy-start | bytes 2359300
